TPU v7x, 32 devices: a whole 2x2x4 slice. The times are simulated.
32 devices in a mesh: seq: 8 (over z, x), kvh: 4 (over y, core).
Axes of the slice: x: 2, y: 2, z: 4, core: 2. Of those that a mesh axis runs over, the one named last changes fastest.
Arguments:
- queries: bfloat16 [4096, 4, 4, 128], P('seq', 'kvh'), may hold values from -12 to 12
- key_states: bfloat16 [4096, 4, 128], P('seq', 'kvh'), may hold values from -10 to 10
- value_states: bfloat16 [4096, 4, 128], P('seq', 'kvh'), may hold values from -4 to 4
- grad_out: bfloat16 [4096, 4, 4, 128], P('seq', 'kvh'), may hold values from -96 to 96
- ancestors: int32 [8, 6], replicated, may hold values from -1 to 6, as said below
- query_weight: bfloat16 [8192, 4, 4, 128], P(None, 'kvh'), may hold values from -0.0625 to 0.0625
- key_weight: bfloat16 [8192, 4, 128], P(None, 'kvh'), may hold values from -0.0625 to 0.0625
- value_weight: bfloat16 [8192, 4, 128], P(None, 'kvh'), may hold values from -0.0625 to 0.0625
Outputs:
- grad_input: bfloat16 [4096, 8192], P(('seq', 'kvh'))
- grad_key: bfloat16 [4096, 4, 128], P('seq', 'kvh')
- grad_value: bfloat16 [4096, 4, 128], P('seq', 'kvh')
Inputs may be any that keep to these rules, and one draw needn't show every extreme that they name: Row b lists the strict ancestor blocks of block b, the root block 0 in slot 0 and one level deeper in each further slot, all below b; the remaining slots hold -1. Block 0 has no ancestors and is an ancestor of every other block; the blocks of every subtree are consecutive; some block has 6 ancestors.
All inputs are finite; a program needn't handle non-finite values.
Results may differ from a plain program's by a relative error of at most 0.015.
Values may be sent and summed in bfloat16 or wider, within the bound.
A program may use at most 128 MiB of HBM per device.

v0:
```python
import jax
import jax.numpy as jnp
from jax import lax
from jax.sharding import PartitionSpec as P

BLOCK = 512
DEPTH = 6


def score_block(query_block, key_block, factor):
    return (
        jnp.einsum("qgd,kd->gqk", query_block, key_block, preferred_element_type=jnp.float32)
        * factor
    )


def local(
    queries, key_states, value_states, grad_out, ancestors, query_weight, key_weight, value_weight
):
    local_rows = queries.shape[0]
    head_count = queries.shape[2]
    head_width = queries.shape[3]
    factor = head_width ** (-0.5)
    query_local = queries[:, 0]
    grad_local = grad_out[:, 0]
    pair_local = jnp.concatenate([key_states, value_states], 1)
    gathered = lax.all_gather(pair_local, "seq", axis=0, tiled=True)
    window = gathered.shape[0]
    block_count = local_rows // BLOCK
    first_block = lax.axis_index("seq") * block_count
    offsets = jnp.arange(BLOCK, dtype=jnp.int32)
    causal = (offsets[:, None] >= offsets[None, :])[None]
    carried = (jnp.zeros((window, 2, head_width), jnp.float32),)

    def deposit(carried, target, contribution):
        row_base = target * BLOCK
        current = lax.dynamic_slice_in_dim(carried[0], row_base, BLOCK, 0)
        return (lax.dynamic_update_slice_in_dim(carried[0], current + contribution, row_base, 0),)

    depth_list = []
    block_id = first_block + 0
    query_block = query_local
    grad_block = grad_local
    listed = lax.dynamic_index_in_dim(ancestors, block_id, 0, keepdims=False)
    depth_here = jnp.sum((listed >= 0).astype(jnp.int32))
    depth_list.append(depth_here)
    slot_total = DEPTH

    def fetch_slot(slot_id, listed=listed):
        target = lax.dynamic_index_in_dim(listed, slot_id, 0, keepdims=False)
        present = target >= 0
        anchor = jnp.maximum(target, 0)
        pair_block = lax.dynamic_slice_in_dim(gathered, anchor * BLOCK, BLOCK, 0)
        return (anchor, present, pair_block)

    def gather_stats(running, pair_block, visible, query_block=query_block, grad_block=grad_block):
        row_peak, total_mass, weighted = running
        scores = jnp.where(visible, score_block(query_block, pair_block[:, 0], factor), -jnp.inf)
        new_peak = jnp.maximum(row_peak, jnp.max(scores, axis=-1, keepdims=True))
        rescale = jnp.exp(row_peak - new_peak)
        exp_terms = jnp.where(visible, jnp.exp(scores - new_peak), 0.0)
        grad_probs = jnp.einsum(
            "qgd,kd->gqk", grad_block, pair_block[:, 1], preferred_element_type=jnp.float32
        )
        total_mass = total_mass * rescale + jnp.sum(exp_terms, axis=-1, keepdims=True)
        weighted = weighted * rescale + jnp.sum(exp_terms * grad_probs, axis=-1, keepdims=True)
        return (new_peak, total_mass, weighted)

    def stats_step(slot_id, running, fetch_slot=fetch_slot, gather_stats=gather_stats):
        anchor, present, pair_block = fetch_slot(slot_id)
        return gather_stats(running, pair_block, present)

    running = (
        jnp.full((head_count, BLOCK, 1), -jnp.inf, jnp.float32),
        jnp.zeros((head_count, BLOCK, 1), jnp.float32),
        jnp.zeros((head_count, BLOCK, 1), jnp.float32),
    )
    running = gather_stats(running, pair_local, causal)
    running = lax.fori_loop(0, slot_total, stats_step, running)
    log_norm = running[0] + jnp.log(running[1])
    delta_row = running[2] / running[1]

    def backward_terms(
        pair_block,
        visible,
        query_block=query_block,
        grad_block=grad_block,
        log_norm=log_norm,
        delta_row=delta_row,
    ):
        scores = score_block(query_block, pair_block[:, 0], factor)
        attn_weight = jnp.where(visible, jnp.exp(scores - log_norm), 0.0)
        grad_probs = jnp.einsum(
            "qgd,kd->gqk", grad_block, pair_block[:, 1], preferred_element_type=jnp.float32
        )
        grad_scores = (attn_weight * (grad_probs - delta_row) * factor).astype(jnp.bfloat16)
        prob_low = attn_weight.astype(jnp.bfloat16)
        query_term = jnp.einsum(
            "gqk,kd->qgd", grad_scores, pair_block[:, 0], preferred_element_type=jnp.float32
        )
        key_term = jnp.einsum(
            "gqk,qgd->kd", grad_scores, query_block, preferred_element_type=jnp.float32
        )
        value_term = jnp.einsum(
            "gqk,qgd->kd", prob_low, grad_block, preferred_element_type=jnp.float32
        )
        return (query_term, jnp.stack([key_term, value_term], 1))

    def grad_step(slot_id, loop_carry, fetch_slot=fetch_slot, backward_terms=backward_terms):
        query_total, inner_carried = loop_carry
        anchor, present, pair_block = fetch_slot(slot_id)
        query_term, pair_term = backward_terms(pair_block, present)
        return (query_total + query_term, deposit(inner_carried, anchor, pair_term))

    query_total, pair_term = backward_terms(pair_local, causal)
    carried = deposit(carried, block_id, pair_term)
    query_total, carried = lax.fori_loop(0, slot_total, grad_step, (query_total, carried))
    query_parts = query_total.astype(jnp.bfloat16)
    pair_grads = lax.psum_scatter(
        carried[0].astype(jnp.bfloat16), "seq", scatter_dimension=0, tiled=True
    )
    flat_query = query_parts.reshape(local_rows, head_count * head_width)
    query_matrix = query_weight[:, 0].reshape(query_weight.shape[0], head_count * head_width)
    key_matrix = key_weight[:, 0]
    value_matrix = value_weight[:, 0]
    contract = (((1,), (1,)), ((), ()))
    key_rows = pair_grads[:, 0]
    value_rows = pair_grads[:, 1]
    result = lax.dot_general(flat_query, query_matrix, contract, preferred_element_type=jnp.float32)
    result = result + lax.dot_general(
        key_rows, key_matrix, contract, preferred_element_type=jnp.float32
    )
    grad_input = lax.psum_scatter(
        (
            result
            + lax.dot_general(
                value_rows, value_matrix, contract, preferred_element_type=jnp.float32
            )
        ).astype(jnp.bfloat16),
        "kvh",
        scatter_dimension=0,
        tiled=True,
    )
    return (grad_input, pair_grads[:, 0:1], pair_grads[:, 1:2])


def solution(mesh):
    return jax.shard_map(
        local,
        mesh=mesh,
        in_specs=(
            P("seq", "kvh", None, None),
            P("seq", "kvh", None),
            P("seq", "kvh", None),
            P("seq", "kvh", None, None),
            P(),
            P(None, "kvh", None, None),
            P(None, "kvh", None),
            P(None, "kvh", None),
        ),
        out_specs=(P(("seq", "kvh"), None), P("seq", "kvh", None), P("seq", "kvh", None)),
        check_vma=False,
    )
```

profile of v0, /device:TPU:0, one launch (start us, length us, event | category | flops | bytes accessed | tf_op | source)
XLA Modules:
  0.0 359.7 jit_solution(15568833139301307411)
XLA Ops:
  10.0 2.0 fusion.36
  12.0 3.6 %fusion.30 = (f32[4,512]{1,0:T(4,128)S(1)}, f32[4,512]{1,0:T(4,128)S(1)}, f32[512,512,4]{1,0,2:T(8,128)}) fusion(f32[512,512,4]{1,0,2:T(8,128)S(1)} %get-tuple-element.360, f32[4,512]{1,0:T(4,128)S(1)} %get-tuple-element.359, pred[512,512]{0,1:T(8,128)(4,1)S(1)} %iota_compare_fusion, bf16[512,1,4,128]{3,2,1,0:T(4,128)(2,1)S(1)} %copy-done.10, ...), kind=kOutput, calls=%fused_computation.47 | convolution fusion | flops 275771392 | bytes 9330688 | tf_op jit(solution)/shard_map/qgd,kd->gqk/dot_general | solution.py:62
  16.6 46.2 %all-gather.2.cloned.1.call-done = bf16[4096,2,128]{2,0,1:T(8,128)(2,1)} async-done(((bf16[512,2,128]{2,0,1:T(8,128)(2,1)}), bf16[4096,2,128]{2,0,1:T(8,128)(2,1)}) %all-gather.2.cloned.1.call-update) | async-done | bytes 2097168 | tf_op jit(solution)/shard_map/all_gather | solution.py:27
  62.8 41.1 %while.32 = (s32[]{:T(128)}, f32[4,512,1]{1,0,2:T(4,128)S(1)}, f32[4,512,1]{1,0,2:T(4,128)S(1)}, f32[4,512,1]{1,0,2:T(4,128)S(1)}, s32[6]{0:T(128)S(1)}, /*index...) while((s32[]{:T(128)}, f32[4,512,1]{1,0,2:T(4,128)S(1)}, ...), condition=%wide.region_7.8_spmd, body=%wide.region_3.7_spmd.sunk | while | flops 551557120 | bytes 16140049 | solution.py:79
  66.4 2.2 fusion.87
  73.3 2.2 fusion.87
  80.1 2.2 fusion.87
  86.9 2.2 fusion.87
  93.8 2.2 fusion.87
  100.6 2.2 fusion.87
  103.9 4.1 %fusion.45 = f32[512,1,128]{2,0,1:T(8,128)} fusion(f32[512,512,4]{1,0,2:T(8,128)} %copy-done.4, f32[4,512]{1,0:T(4,128)S(1)} %bitcast.256, pred[512,512]{0,1:T(8,128)(4,1)S(1)} %iota_compare_fusion, bf16[512,1,4,128]{3,2,1,0:T(4,128)(2,1)} %param.15), kind=kOutput, calls=%fused_computation.65 | convolution fusion | flops 272629760 | bytes 5251072 | tf_op jit(solution)/shard_map/gqk,qgd->kd/dot_general | solution.py:104
  108.0 3.6 fusion.33
  114.7 2.6 copy.16
  120.2 66.6 %while.33 = (s32[]{:T(128)}, f32[512,4,128]{0,2,1:T(8,128)}, f32[4096,2,128]{2,0,1:T(8,128)}, s32[6]{0:T(128)S(1)}, bf16[4096,2,128]{2,0,1:T(8,128)(2,1)}, /*ind...) while((s32[]{:T(128)}, f32[512,4,128]{0,2,1:T(8,128)}, ...), condition=%wide.region_9.10_spmd, body=%wide.region_8.9_spmd.sunk | while | flops 1354235904 | bytes 33973052 | solution.py:117
  124.6 2.4 fusion.97
  129.0 2.3 fusion.100
  135.6 2.4 fusion.97
  140.2 2.3 fusion.100
  146.8 2.4 fusion.97
  151.2 2.3 fusion.100
  157.8 2.4 fusion.97
  162.3 2.3 fusion.100
  168.9 2.4 fusion.97
  173.4 2.3 fusion.100
  180.0 2.4 fusion.97
  184.5 2.3 fusion.100
  186.8 3.8 %convert_element_type.32 = bf16[4096,2,128]{2,0,1:T(8,128)(2,1)} convert(f32[4096,2,128]{2,0,1:T(8,128)} %get-tuple-element.303) | non-fusion elementwise | flops 1048576 | bytes 6291456 | tf_op jit(solution)/shard_map/convert_element_type | solution.py:120
  192.0 11.8 %fusion.27 = f32[512,8192]{1,0:T(8,128)} fusion(bf16[512,512]{0,1:T(8,128)(2,1)S(1)} %bitcast.254, bf16[1024,8,4,128]{3,2,1,0:T(4,128)(2,1)} %bitcast.251), kind=kOutput, calls=%fused_computation.42 | convolution fusion | flops 4294967296 | bytes 25690112 | tf_op jit(solution)/shard_map/dot_general | solution.py:129
  203.8 53.5 %reduce-scatter.3.cloned.1.call-done = bf16[512,2,128]{2,0,1:T(8,128)(2,1)} async-done(((bf16[4096,2,128]{2,0,1:T(8,128)(2,1)}), bf16[512,2,128]{2,0,1:T(8,128)(2,1)}) %reduce-scatter.3.cloned.1.call-update) | async-done | bytes 262160 | tf_op jit(solution)/shard_map/reduce_scatter | solution.py:119
  258.3 8.1 %fusion.40 = f32[512,8192]{1,0:T(8,128)} fusion(bf16[8192,1,128]{2,0,1:T(8,128)(2,1)S(1)} %copy-done, bf16[512,1,128]{2,0,1:T(8,128)(2,1)S(1)} %get-tuple-element.354), kind=kOutput, calls=%fused_computation.60 | convolution fusion | flops 1073741824 | bytes 19005440 | tf_op jit(solution)/shard_map/dot_general | solution.py:130
  266.4 15.9 %add_convert_fusion = bf16[512,8192]{1,0:T(8,128)(2,1)} fusion(f32[512,8192]{1,0:T(8,128)} %fusion.27, f32[512,8192]{1,0:T(8,128)} %fusion.40, bf16[8192,1,128]{2,0,1:T(8,128)(2,1)} %param.19, bf16[512,1,128]{2,0,1:T(8,128)(2,1)S(1)} %get-tuple-element.353), kind=kOutput, calls=%fused_computation.41 | convolution fusion | flops 1086324736 | bytes 44171264 | tf_op jit(solution)/shard_map/dot_general | solution.py:136
  282.3 70.9 %reduce-scatter.5.cloned.1.call-done = bf16[128,8192]{1,0:T(8,128)(2,1)} async-done(((bf16[512,8192]{1,0:T(8,128)(2,1)}), bf16[128,8192]{1,0:T(8,128)(2,1)}) %reduce-scatter.5.cloned.1.call-update) | async-done | bytes 2097168 | tf_op jit(solution)/shard_map/reduce_scatter | solution.py:133
  (148 shorter events, 62.0 us)
Async XLA Ops:
  7.2 251.2 %copy-start = (bf16[8192,1,128]{2,0,1:T(8,128)(2,1)S(1)}, bf16[8192,1,128]{2,0,1:T(8,128)(2,1)}, u32[]{:S(2)}) copy-start(bf16[8192,1,128]{2,0,1:T(8,128)(2,1)} %param.18) | copy-start | bytes 6291460
  7.2 4.8 %copy-start.16 = (bf16[512,1,128]{2,0,1:T(8,128)(2,1)S(1)}, bf16[512,1,128]{2,0,1:T(8,128)(2,1)}, u32[]{:S(2)}) copy-start(bf16[512,1,128]{2,0,1:T(8,128)(2,1)} %param.14) | copy-start | bytes 393220
  7.2 4.8 %copy-start.10 = (bf16[512,1,4,128]{3,2,1,0:T(4,128)(2,1)S(1)}, bf16[512,1,4,128]{3,2,1,0:T(4,128)(2,1)}, u32[]{:S(2)}) copy-start(bf16[512,1,4,128]{3,2,1,0:T(4,128)(2,1)} %param.15) | copy-start | bytes 1572868
  7.2 55.6 %all-gather.2.cloned.1.call-start = ((), (), s32[]{:S(2)}) async-start(), calls=%async_computation.2 | async-start | bytes 2359296 | tf_op jit(solution)/shard_map/all_gather | solution.py:27
  9.1 248.2 %reduce-scatter.3.cloned.1.call-start = ((), (), s32[]{:S(2)}) async-start(), calls=%async_computation.3 | async-start | bytes 2359296 | tf_op jit(solution)/shard_map/reduce_scatter | solution.py:119
  12.0 3.7 %copy-start.4 = (f32[512,512,4]{1,0,2:T(8,128)}, f32[512,512,4]{1,0,2:T(8,128)S(1)}, u32[]{:S(2)}) copy-start(f32[512,512,4]{1,0,2:T(8,128)S(1)} %get-tuple-element.360) | copy-start | bytes 12582916
  12.0 3.7 %copy-start.6 = (bf16[512,1,4,128]{3,2,1,0:T(4,128)(2,1)S(1)}, bf16[512,1,4,128]{3,2,1,0:T(4,128)(2,1)}, u32[]{:S(2)}) copy-start(bf16[512,1,4,128]{3,2,1,0:T(4,128)(2,1)} %param.12) | copy-start | bytes 1572868
  12.0 3.7 %copy-start.11 = (bf16[512,1,4,128]{3,2,1,0:T(4,128)(2,1)S(1)}, bf16[512,1,4,128]{3,2,1,0:T(4,128)(2,1)}, u32[]{:S(2)}) copy-start(bf16[512,1,4,128]{3,2,1,0:T(4,128)(2,1)} %param.15) | copy-start | bytes 1572868
  64.0 2.4 copy-start.12
  70.9 2.4 copy-start.12
  77.7 2.4 copy-start.12
  84.6 2.4 copy-start.12
  91.4 2.4 copy-start.12
  98.3 2.4 copy-start.12
  103.9 4.1 %copy-start.5 = (f32[512,512,4]{1,0,2:T(8,128)S(1)}, f32[512,512,4]{1,0,2:T(8,128)}, u32[]{:S(2)}) copy-start(f32[512,512,4]{1,0,2:T(8,128)} %copy-done.4) | copy-start | bytes 12582916
  108.0 5.0 %copy-start.7 = (bf16[512,1,128]{2,0,1:T(8,128)(2,1)S(1)}, bf16[512,1,128]{2,0,1:T(8,128)(2,1)}, u32[]{:S(2)}) copy-start(bf16[512,1,128]{2,0,1:T(8,128)(2,1)} %param.13) | copy-start | bytes 393220
  113.0 4.6 %copy-start.14 = (f32[512,1,128]{2,0,1:T(8,128)S(1)}, f32[512,1,128]{2,0,1:T(8,128)}, u32[]{:S(2)}) copy-start(f32[512,1,128]{2,0,1:T(8,128)} %fusion.45) | copy-start | bytes 786436
  114.7 5.6 %copy-start.13 = (bf16[512,4,128]{2,0,1:T(8,128)(2,1)S(1)}, bf16[512,4,128]{2,0,1:T(8,128)(2,1)}, u32[]{:S(2)}) copy-start(bf16[512,4,128]{2,0,1:T(8,128)(2,1)} %get-tuple-element.575) | copy-start | bytes 1572868
  124.5 3.1 copy-start.1
  129.0 2.3 copy-start.2
  135.6 3.1 copy-start.1
  140.1 2.3 copy-start.2
  146.7 3.1 copy-start.1
  151.2 2.3 copy-start.2
  157.8 3.1 copy-start.1
  162.3 2.3 copy-start.2
  168.9 3.1 copy-start.1
  173.4 2.3 copy-start.2
  180.0 3.1 copy-start.1
  190.6 162.5 %reduce-scatter.5.cloned.1.call-start = ((), (), s32[]{:S(2)}) async-start(), calls=%async_computation.4 | async-start | bytes 10485760 | tf_op jit(solution)/shard_map/reduce_scatter | solution.py:133
  258.3 8.1 %copy-start.9 = (bf16[512,1,128]{2,0,1:T(8,128)(2,1)}, bf16[512,1,128]{2,0,1:T(8,128)(2,1)S(1)}, u32[]{:S(2)}) copy-start(bf16[512,1,128]{2,0,1:T(8,128)(2,1)S(1)} %get-tuple-element.354) | copy-start | bytes 393220
  258.3 8.1 %copy-start.8 = (bf16[512,1,128]{2,0,1:T(8,128)(2,1)}, bf16[512,1,128]{2,0,1:T(8,128)(2,1)S(1)}, u32[]{:S(2)}) copy-start(bf16[512,1,128]{2,0,1:T(8,128)(2,1)S(1)} %get-tuple-element.353) | copy-start | bytes 393220
  (3 other events, 5.2 us)
Sparse Core Ops, SparseCore 0:
  10.8 51.9 all-gather.1
  190.8 66.4 reduce-scatter.2
  282.4 70.7 reduce-scatter.4
where the time goes:
time: 361 us; the launch traced here: 360 us
  waiting for transfers between devices  171 us (47%)
  matrix products  113 us (31%)
  other arithmetic  30.4 us (8%)
  loops' own time  16.7 us (5%)
  local copies, waits for them, and re-layouts  15.3 us (4%)
  between operations  13.9 us (4%)
    reduce_scatter x1, waiting for transfers between devices, local(): lax.psum_scatter((result + lax.dot_general(value_rows, value_matrix, cont...  70.9 us
    reduce_scatter x1, waiting for transfers between devices, local(): lax.psum_scatter(carried[0].astype(jnp.bfloat16), 'seq', scatter_dimensio...  53.5 us
    all_gather x1, waiting for transfers between devices, local(): gathered = lax.all_gather(pair_local, 'seq', axis=0, tiled=True)  46.2 us
    dot_general x13, matrix products, score_block(): jnp.einsum('qgd,kd->gqk', query_block, key_block, preferred_element_type=...  21.5 us
    dot_general x7, matrix products, gather_stats(): jnp.einsum('qgd,kd->gqk', grad_block, pair_block[:, 1], preferred_element...  16.8 us
    dot_general x1, matrix products, local(): lax.dot_general(value_rows, value_matrix, contract, preferred_element_typ...  15.9 us
    dot_general x6, matrix products, backward_terms(): jnp.einsum('qgd,kd->gqk', grad_block, pair_block[:, 1], preferred_element...  14.2 us
    dynamic_update_slice x7, other arithmetic, deposit(): lax.dynamic_update_slice_in_dim(carried[0], current + contribution, row_b...  13.8 us
  transfers between devices with their start and end apart: 3, of which 3 were waited for; matrix products, arithmetic and copies ran while one was open for 6% of the time, Pallas kernels for 0%

commit v1 on v0

--- a/solution.py
+++ b/solution.py
@@ -24,7 +24,12 @@
     query_local = queries[:, 0]
     grad_local = grad_out[:, 0]
     pair_local = jnp.concatenate([key_states, value_states], 1)
-    gathered = lax.all_gather(pair_local, "seq", axis=0, tiled=True)
+    ring = [pair_local]
+    for hop in range(7):
+        ring.append(lax.ppermute(ring[-1], "seq", [(dev, (dev + 1) % 8) for dev in range(8)]))
+    gathered = jnp.roll(
+        jnp.concatenate(ring[::-1], axis=0), (lax.axis_index("seq") + 1) * ring[0].shape[0], axis=0
+    )
     window = gathered.shape[0]
     block_count = local_rows // BLOCK
     first_block = lax.axis_index("seq") * block_count

time: 361 us -> 393 us (1.089)
  local copies, waits for them, and re-layouts: 15.3 us -> 33.6 us
  waiting for transfers between devices: 171 us -> 179 us
    ppermute x0 -> x7, waiting for transfers between devices: none -> 54.8 us  [local(): lax.ppermute(ring[-1], 'seq', [(dev, (dev + 1) % 8) for dev in range(8)])]
    all_gather x1 -> x0, waiting for transfers between devices: 46.2 us -> none  [local(): gathered = lax.all_gather(pair_local, 'seq', axis=0, tiled=True)]
    unnamed x28 -> x73, local copies, waits for them, and re-layouts: 2.67 us -> 10.6 us
  transfers between devices with their start and end apart: 3 -> 9, of which waited for: 3 -> 9; matrix products, arithmetic and copies ran while one was open for 6% -> 6% of each run, Pallas kernels for 0% -> 0%
where the time goes in v1:
time: 393 us; the launch traced here: 391 us
  waiting for transfers between devices  179 us (46%)
  matrix products  114 us (29%)
  local copies, waits for them, and re-layouts  33.6 us (9%)
  other arithmetic  30.8 us (8%)
  loops' own time  16.8 us (4%)
  between operations  14.4 us (4%)
    reduce_scatter x1, waiting for transfers between devices, local(): lax.psum_scatter((result + lax.dot_general(value_rows, value_matrix, cont...  70.8 us
    ppermute x7, waiting for transfers between devices, local(): lax.ppermute(ring[-1], 'seq', [(dev, (dev + 1) % 8) for dev in range(8)])  54.8 us
    reduce_scatter x1, waiting for transfers between devices, local(): lax.psum_scatter(carried[0].astype(jnp.bfloat16), 'seq', scatter_dimensio...  53.2 us
    dot_general x13, matrix products, score_block(): jnp.einsum('qgd,kd->gqk', query_block, key_block, preferred_element_type=...  21.6 us
    dot_general x7, matrix products, gather_stats(): jnp.einsum('qgd,kd->gqk', grad_block, pair_block[:, 1], preferred_element...  17.4 us
    dot_general x1, matrix products, local(): lax.dot_general(value_rows, value_matrix, contract, preferred_element_typ...  15.9 us
    dot_general x6, matrix products, backward_terms(): jnp.einsum('qgd,kd->gqk', grad_block, pair_block[:, 1], preferred_element...  14.3 us
    dynamic_update_slice x7, other arithmetic, deposit(): lax.dynamic_update_slice_in_dim(carried[0], current + contribution, row_b...  13.9 us
  transfers between devices with their start and end apart: 9, of which 9 were waited for; matrix products, arithmetic and copies ran while one was open for 6% of the time, Pallas kernels for 0%

profile of v1, /device:TPU:0, one launch (start us, length us, event | category | flops | bytes accessed | tf_op | source)
XLA Modules:
  0.0 391.3 jit_solution(357269059996937770)
XLA Ops:
  8.4 3.0 collective-permute-start
  11.4 9.3 %collective-permute-done = bf16[512,2,128]{2,0,1:T(8,128)(2,1)S(1)} collective-permute-done((bf16[512,2,128]{2,0,1:T(8,128)(2,1)S(1)}, bf16[512,2,128]{2,0,1:T(8,128)(2,1)S(1)}, u32[]{:S(2)}, u32[]{:S(2)}) %collective-permute-start) | collective-permute-done | bytes 262176 | tf_op jit(solution)/shard_map/ppermute | solution.py:29
  21.4 10.2 %collective-permute-done.1 = bf16[512,2,128]{2,0,1:T(8,128)(2,1)S(1)} collective-permute-done((bf16[512,2,128]{2,0,1:T(8,128)(2,1)S(1)}, bf16[512,2,128]{2,0,1:T(8,128)(2,1)S(1)}, u32[]{:S(2)}, u32[]{:S(2)}) %collective-permute-start.1) | collective-permute-done | bytes 262176 | tf_op jit(solution)/shard_map/ppermute | solution.py:29
  31.7 9.2 %collective-permute-done.2 = bf16[512,2,128]{2,0,1:T(8,128)(2,1)S(1)} collective-permute-done((bf16[512,2,128]{2,0,1:T(8,128)(2,1)S(1)}, bf16[512,2,128]{2,0,1:T(8,128)(2,1)S(1)}, u32[]{:S(2)}, u32[]{:S(2)}) %collective-permute-start.2) | collective-permute-done | bytes 262176 | tf_op jit(solution)/shard_map/ppermute | solution.py:29
  43.0 7.0 %collective-permute-done.3 = bf16[512,2,128]{2,0,1:T(8,128)(2,1)S(1)} collective-permute-done((bf16[512,2,128]{2,0,1:T(8,128)(2,1)S(1)}, bf16[512,2,128]{2,0,1:T(8,128)(2,1)S(1)}, u32[]{:S(2)}, u32[]{:S(2)}) %collective-permute-start.3) | collective-permute-done | bytes 262176 | tf_op jit(solution)/shard_map/ppermute | solution.py:29
  50.0 4.3 %fusion.30 = (f32[4,512]{1,0:T(4,128)}, f32[4,512]{1,0:T(4,128)}, f32[512,512,4]{1,0,2:T(8,128)}) fusion(f32[512,512,4]{1,0,2:T(8,128)S(1)} %get-tuple-element.360, f32[4,512]{1,0:T(4,128)S(1)} %get-tuple-element.359, pred[512,512]{0,1:T(8,128)(4,1)S(1)} %iota_compare_fusion, bf16[512,1,4,128]{3,2,1,0:T(4,128)(2,1)S(1)} %copy-done.21, ...), kind=kOutput, calls=%fused_computation.47 | convolution fusion | flops 275771392 | bytes 9330688 | tf_op jit(solution)/shard_map/qgd,kd->gqk/dot_general | solution.py:67
  54.3 4.8 %collective-permute-done.4 = bf16[512,2,128]{2,0,1:T(8,128)(2,1)} collective-permute-done((bf16[512,2,128]{2,0,1:T(8,128)(2,1)S(1)}, bf16[512,2,128]{2,0,1:T(8,128)(2,1)}, u32[]{:S(2)}, u32[]{:S(2)}) %collective-permute-start.4) | collective-permute-done | bytes 262176 | tf_op jit(solution)/shard_map/ppermute | solution.py:29
  61.8 7.1 %collective-permute-done.5 = bf16[512,2,128]{2,0,1:T(8,128)(2,1)} collective-permute-done((bf16[512,2,128]{2,0,1:T(8,128)(2,1)}, bf16[512,2,128]{2,0,1:T(8,128)(2,1)}, u32[]{:S(2)}, u32[]{:S(2)}) %collective-permute-start.5) | collective-permute-done | bytes 262176 | tf_op jit(solution)/shard_map/ppermute | solution.py:29
  70.9 7.2 %collective-permute-done.6 = bf16[512,2,128]{2,0,1:T(8,128)(2,1)S(1)} collective-permute-done((bf16[512,2,128]{2,0,1:T(8,128)(2,1)}, bf16[512,2,128]{2,0,1:T(8,128)(2,1)S(1)}, u32[]{:S(2)}, u32[]{:S(2)}) %collective-permute-start.6) | collective-permute-done | bytes 262176 | tf_op jit(solution)/shard_map/ppermute | solution.py:29
  86.9 48.4 %while.32 = (s32[]{:T(128)}, f32[4,512,1]{1,0,2:T(4,128)S(1)}, f32[4,512,1]{1,0,2:T(4,128)}, f32[4,512,1]{1,0,2:T(4,128)S(1)}, s32[6]{0:T(128)}, /*index=5*/bf16...) while((s32[]{:T(128)}, f32[4,512,1]{1,0,2:T(4,128)S(1)}, ...), condition=%wide.region_7.8_spmd, body=%wide.region_3.7_spmd.sunk | while | flops 551557120 | bytes 16205641 | solution.py:84
  136.2 4.2 %fusion.45 = f32[512,1,128]{2,0,1:T(8,128)} fusion(f32[512,512,4]{1,0,2:T(8,128)} %copy-done.5, f32[4,512]{1,0:T(4,128)S(1)} %bitcast.256, pred[512,512]{0,1:T(8,128)(4,1)S(1)} %iota_compare_fusion, bf16[512,1,4,128]{3,2,1,0:T(4,128)(2,1)} %param.15), kind=kOutput, calls=%fused_computation.65 | convolution fusion | flops 272629760 | bytes 5251072 | tf_op jit(solution)/shard_map/gqk,qgd->kd/dot_general | solution.py:109
  140.3 3.5 fusion.33
  147.1 2.6 copy.16
  152.7 66.8 %while.33 = (s32[]{:T(128)}, f32[512,4,128]{0,2,1:T(8,128)}, f32[4096,2,128]{2,0,1:T(8,128)}, s32[6]{0:T(128)S(1)}, bf16[4096,2,128]{2,0,1:T(8,128)(2,1)}, /*ind...) while((s32[]{:T(128)}, f32[512,4,128]{0,2,1:T(8,128)}, ...), condition=%wide.region_9.10_spmd, body=%wide.region_8.9_spmd.sunk | while | flops 1354235904 | bytes 33973052 | solution.py:122
  157.0 2.4 fusion.98
  161.5 2.3 fusion.101
  168.1 2.4 fusion.98
  172.6 2.3 fusion.101
  179.3 2.4 fusion.98
  183.8 2.3 fusion.101
  190.4 2.4 fusion.98
  194.9 2.3 fusion.101
  201.5 2.4 fusion.98
  206.0 2.3 fusion.101
  212.7 2.4 fusion.98
  217.2 2.3 fusion.101
  219.5 3.9 convert_element_type.32
  223.5 11.8 %fusion.27 = f32[512,8192]{1,0:T(8,128)} fusion(bf16[512,512]{0,1:T(8,128)(2,1)S(1)} %bitcast.254, bf16[1024,8,4,128]{3,2,1,0:T(4,128)(2,1)} %bitcast.251), kind=kOutput, calls=%fused_computation.42 | convolution fusion | flops 4294967296 | bytes 25690112 | tf_op jit(solution)/shard_map/dot_general | solution.py:134
  235.3 53.2 %reduce-scatter.3.cloned.1.call-done = bf16[512,2,128]{2,0,1:T(8,128)(2,1)} async-done(((bf16[4096,2,128]{2,0,1:T(8,128)(2,1)}), bf16[512,2,128]{2,0,1:T(8,128)(2,1)}) %reduce-scatter.3.cloned.1.call-update) | async-done | bytes 262160 | tf_op jit(solution)/shard_map/reduce_scatter | solution.py:124
  289.6 8.1 %fusion.40 = f32[512,8192]{1,0:T(8,128)} fusion(bf16[8192,1,128]{2,0,1:T(8,128)(2,1)S(1)} %copy-done, bf16[512,1,128]{2,0,1:T(8,128)(2,1)S(1)} %get-tuple-element.354), kind=kOutput, calls=%fused_computation.60 | convolution fusion | flops 1073741824 | bytes 19005440 | tf_op jit(solution)/shard_map/dot_general | solution.py:135
  297.7 15.9 %add_convert_fusion = bf16[512,8192]{1,0:T(8,128)(2,1)} fusion(f32[512,8192]{1,0:T(8,128)} %fusion.27, f32[512,8192]{1,0:T(8,128)} %fusion.40, bf16[8192,1,128]{2,0,1:T(8,128)(2,1)} %param.19, bf16[512,1,128]{2,0,1:T(8,128)(2,1)S(1)} %get-tuple-element.353), kind=kOutput, calls=%fused_computation.41 | convolution fusion | flops 1086324736 | bytes 44171264 | tf_op jit(solution)/shard_map/dot_general | solution.py:141
  313.6 70.8 %reduce-scatter.5.cloned.1.call-done = bf16[128,8192]{1,0:T(8,128)(2,1)} async-done(((bf16[512,8192]{1,0:T(8,128)(2,1)}), bf16[128,8192]{1,0:T(8,128)(2,1)}) %reduce-scatter.5.cloned.1.call-update) | async-done | bytes 2097168 | tf_op jit(solution)/shard_map/reduce_scatter | solution.py:138
  (230 shorter events, 95.8 us)
Async XLA Ops:
  7.2 282.4 %copy-start = (bf16[8192,1,128]{2,0,1:T(8,128)(2,1)S(1)}, bf16[8192,1,128]{2,0,1:T(8,128)(2,1)}, u32[]{:S(2)}) copy-start(bf16[8192,1,128]{2,0,1:T(8,128)(2,1)} %param.18) | copy-start | bytes 6291460
  7.2 42.8 %copy-start.9 = (bf16[512,1,128]{2,0,1:T(8,128)(2,1)S(1)}, bf16[512,1,128]{2,0,1:T(8,128)(2,1)}, u32[]{:S(2)}) copy-start(bf16[512,1,128]{2,0,1:T(8,128)(2,1)} %param.14) | copy-start | bytes 393220
  7.2 281.4 %reduce-scatter.3.cloned.1.call-start = ((), (), s32[]{:S(2)}) async-start(), calls=%async_computation.2 | async-start | bytes 2359296 | tf_op jit(solution)/shard_map/reduce_scatter | solution.py:124
  8.4 12.3 %collective-permute-start = (bf16[512,2,128]{2,0,1:T(8,128)(2,1)S(1)}, bf16[512,2,128]{2,0,1:T(8,128)(2,1)S(1)}, u32[]{:S(2)}, u32[]{:S(2)}) collective-permute-start(bf16[512,2,128]{2,0,1:T(8,128)(2,1)S(1)} %pad_maximum_fusion), channel_id=1, source_target_pairs={{0,4},{4,8},{8,12},{12,16},{16,20},{20,24},{24,28},{28,0},{1,5},{5... | collective-permute-start | bytes 786440 | tf_op jit(solution)/shard_map/ppermute | solution.py:29
  21.4 10.2 %collective-permute-start.1 = (bf16[512,2,128]{2,0,1:T(8,128)(2,1)S(1)}, bf16[512,2,128]{2,0,1:T(8,128)(2,1)S(1)}, u32[]{:S(2)}, u32[]{:S(2)}) collective-permute-start(bf16[512,2,128]{2,0,1:T(8,128)(2,1)S(1)} %collective-permute-done), channel_id=1, source_target_pairs={{0,4},{4,8},{8,12},{12,16},{16,20},{20,24},{24,28},{28,0},{1,5},{5... | collective-permute-start | bytes 786440 | tf_op jit(solution)/shard_map/ppermute | solution.py:29
  31.6 22.7 %copy-start.13 = (bf16[512,2,128]{2,0,1:T(8,128)(2,1)}, bf16[512,2,128]{2,0,1:T(8,128)(2,1)S(1)}, u32[]{:S(2)}) copy-start(bf16[512,2,128]{2,0,1:T(8,128)(2,1)S(1)} %collective-permute-done.1) | copy-start | bytes 786436
  31.6 9.3 %collective-permute-start.2 = (bf16[512,2,128]{2,0,1:T(8,128)(2,1)S(1)}, bf16[512,2,128]{2,0,1:T(8,128)(2,1)S(1)}, u32[]{:S(2)}, u32[]{:S(2)}) collective-permute-start(bf16[512,2,128]{2,0,1:T(8,128)(2,1)S(1)} %collective-permute-done.1), channel_id=1, source_target_pairs={{0,4},{4,8},{8,12},{12,16},{16,20},{20,24},{24,28},{28,0},{1,5},{5... | collective-permute-start | bytes 786440 | tf_op jit(solution)/shard_map/ppermute | solution.py:29
  31.6 18.4 %copy-start.21 = (bf16[512,1,4,128]{3,2,1,0:T(4,128)(2,1)S(1)}, bf16[512,1,4,128]{3,2,1,0:T(4,128)(2,1)}, u32[]{:S(2)}) copy-start(bf16[512,1,4,128]{3,2,1,0:T(4,128)(2,1)} %param.15) | copy-start | bytes 1572868
  40.9 9.1 %copy-start.15 = (bf16[512,2,128]{2,0,1:T(8,128)(2,1)}, bf16[512,2,128]{2,0,1:T(8,128)(2,1)S(1)}, u32[]{:S(2)}) copy-start(bf16[512,2,128]{2,0,1:T(8,128)(2,1)S(1)} %collective-permute-done.2) | copy-start | bytes 786436
  40.9 9.1 %collective-permute-start.3 = (bf16[512,2,128]{2,0,1:T(8,128)(2,1)S(1)}, bf16[512,2,128]{2,0,1:T(8,128)(2,1)S(1)}, u32[]{:S(2)}, u32[]{:S(2)}) collective-permute-start(bf16[512,2,128]{2,0,1:T(8,128)(2,1)S(1)} %collective-permute-done.2), channel_id=1, source_target_pairs={{0,4},{4,8},{8,12},{12,16},{16,20},{20,24},{24,28},{28,0},{1,5},{5... | collective-permute-start | bytes 786440 | tf_op jit(solution)/shard_map/ppermute | solution.py:29
  43.0 11.3 %copy-start.5 = (f32[512,512,4]{1,0,2:T(8,128)}, f32[512,512,4]{1,0,2:T(8,128)S(1)}, u32[]{:S(2)}) copy-start(f32[512,512,4]{1,0,2:T(8,128)S(1)} %get-tuple-element.360) | copy-start | bytes 12582916
  50.0 9.2 %collective-permute-start.4 = (bf16[512,2,128]{2,0,1:T(8,128)(2,1)S(1)}, bf16[512,2,128]{2,0,1:T(8,128)(2,1)}, u32[]{:S(2)}, u32[]{:S(2)}) collective-permute-start(bf16[512,2,128]{2,0,1:T(8,128)(2,1)S(1)} %collective-permute-done.3), channel_id=1, source_target_pairs={{0,4},{4,8},{8,12},{12,16},{16,20},{20,24},{24,28},{28,0},{1,5},{5... | collective-permute-start | bytes 786440 | tf_op jit(solution)/shard_map/ppermute | solution.py:29
  50.0 18.9 %copy-start.8 = (bf16[512,1,4,128]{3,2,1,0:T(4,128)(2,1)S(1)}, bf16[512,1,4,128]{3,2,1,0:T(4,128)(2,1)}, u32[]{:S(2)}) copy-start(bf16[512,1,4,128]{3,2,1,0:T(4,128)(2,1)} %param.12) | copy-start | bytes 1572868
  54.3 27.9 %copy-start.7 = (bf16[512,1,128]{2,0,1:T(8,128)(2,1)S(1)}, bf16[512,1,128]{2,0,1:T(8,128)(2,1)}, u32[]{:S(2)}) copy-start(bf16[512,1,128]{2,0,1:T(8,128)(2,1)} %param.13) | copy-start | bytes 393220
  59.1 9.7 %collective-permute-start.5 = (bf16[512,2,128]{2,0,1:T(8,128)(2,1)}, bf16[512,2,128]{2,0,1:T(8,128)(2,1)}, u32[]{:S(2)}, u32[]{:S(2)}) collective-permute-start(bf16[512,2,128]{2,0,1:T(8,128)(2,1)} %collective-permute-done.4), channel_id=1, source_target_pairs={{0,4},{4,8},{8,12},{12,16},{16,20},{20,24},{24,28},{28,0},{1,5},{5... | collective-permute-start | bytes 786440 | tf_op jit(solution)/shard_map/ppermute | solution.py:29
  60.4 20.8 %copy-start.16 = (bf16[512,2,128]{2,0,1:T(8,128)(2,1)S(1)}, bf16[512,2,128]{2,0,1:T(8,128)(2,1)}, u32[]{:S(2)}) copy-start(bf16[512,2,128]{2,0,1:T(8,128)(2,1)} %copy-done.15) | copy-start | bytes 786436
  60.4 20.8 %copy-start.14 = (bf16[512,2,128]{2,0,1:T(8,128)(2,1)S(1)}, bf16[512,2,128]{2,0,1:T(8,128)(2,1)}, u32[]{:S(2)}) copy-start(bf16[512,2,128]{2,0,1:T(8,128)(2,1)} %copy-done.13) | copy-start | bytes 786436
  60.4 24.8 %copy-start.18 = (bf16[512,2,128]{2,0,1:T(8,128)(2,1)S(1)}, bf16[512,2,128]{2,0,1:T(8,128)(2,1)}, u32[]{:S(2)}) copy-start(bf16[512,2,128]{2,0,1:T(8,128)(2,1)} %copy-done.17) | copy-start | bytes 786436
  68.9 9.3 %collective-permute-start.6 = (bf16[512,2,128]{2,0,1:T(8,128)(2,1)}, bf16[512,2,128]{2,0,1:T(8,128)(2,1)S(1)}, u32[]{:S(2)}, u32[]{:S(2)}) collective-permute-start(bf16[512,2,128]{2,0,1:T(8,128)(2,1)} %collective-permute-done.5), channel_id=1, source_target_pairs={{0,4},{4,8},{8,12},{12,16},{16,20},{20,24},{24,28},{28,0},{1,5},{5... | collective-permute-start | bytes 786440 | tf_op jit(solution)/shard_map/ppermute | solution.py:29
  70.9 14.4 %copy-start.12 = (bf16[512,2,128]{2,0,1:T(8,128)(2,1)S(1)}, bf16[512,2,128]{2,0,1:T(8,128)(2,1)}, u32[]{:S(2)}) copy-start(bf16[512,2,128]{2,0,1:T(8,128)(2,1)} %copy-done.11) | copy-start | bytes 786436
  70.9 14.5 %copy-start.10 = (bf16[512,1,128]{2,0,1:T(8,128)(2,1)S(1)}, bf16[512,1,128]{2,0,1:T(8,128)(2,1)}, u32[]{:S(2)}) copy-start(bf16[512,1,128]{2,0,1:T(8,128)(2,1)} %param.14) | copy-start | bytes 393220
  135.3 5.0 %copy-start.6 = (f32[512,512,4]{1,0,2:T(8,128)S(1)}, f32[512,512,4]{1,0,2:T(8,128)}, u32[]{:S(2)}) copy-start(f32[512,512,4]{1,0,2:T(8,128)} %copy-done.5) | copy-start | bytes 12582916
  136.2 7.7 %copy-start.28 = (f32[4,512,1]{1,0,2:T(4,128)}, f32[4,512,1]{1,0,2:T(4,128)S(1)}, u32[]{:S(2)}) copy-start(f32[4,512,1]{1,0,2:T(4,128)S(1)} %get-tuple-element.524) | copy-start | bytes 24580
  136.2 7.7 %copy-start.30 = (f32[4,512,1]{1,0,2:T(4,128)}, f32[4,512,1]{1,0,2:T(4,128)S(1)}, u32[]{:S(2)}) copy-start(f32[4,512,1]{1,0,2:T(4,128)S(1)} %get-tuple-element.526) | copy-start | bytes 24580
  145.3 4.7 %copy-start.26 = (f32[512,1,128]{2,0,1:T(8,128)S(1)}, f32[512,1,128]{2,0,1:T(8,128)}, u32[]{:S(2)}) copy-start(f32[512,1,128]{2,0,1:T(8,128)} %fusion.45) | copy-start | bytes 786436
  147.0 5.6 %copy-start.23 = (bf16[512,4,128]{2,0,1:T(8,128)(2,1)S(1)}, bf16[512,4,128]{2,0,1:T(8,128)(2,1)}, u32[]{:S(2)}) copy-start(bf16[512,4,128]{2,0,1:T(8,128)(2,1)} %get-tuple-element.580) | copy-start | bytes 1572868
  147.0 5.6 %copy-start.29 = (f32[4,512,1]{1,0,2:T(4,128)S(1)}, f32[4,512,1]{1,0,2:T(4,128)}, u32[]{:S(2)}) copy-start(f32[4,512,1]{1,0,2:T(4,128)} %copy-done.28) | copy-start | bytes 24580
  147.0 5.6 %copy-start.31 = (f32[4,512,1]{1,0,2:T(4,128)S(1)}, f32[4,512,1]{1,0,2:T(4,128)}, u32[]{:S(2)}) copy-start(f32[4,512,1]{1,0,2:T(4,128)} %copy-done.30) | copy-start | bytes 24580
  147.0 5.6 %copy-start.32 = (s32[6]{0:T(128)S(1)}, s32[6]{0:T(128)}, u32[]{:S(2)}) copy-start(s32[6]{0:T(128)} %get-tuple-element.584) | copy-start | bytes 76
  223.4 161.1 %reduce-scatter.5.cloned.1.call-start = ((), (), s32[]{:S(2)}) async-start(), calls=%async_computation.3 | async-start | bytes 10485760 | tf_op jit(solution)/shard_map/reduce_scatter | solution.py:138
  289.5 8.1 %copy-start.20 = (bf16[512,1,128]{2,0,1:T(8,128)(2,1)}, bf16[512,1,128]{2,0,1:T(8,128)(2,1)S(1)}, u32[]{:S(2)}) copy-start(bf16[512,1,128]{2,0,1:T(8,128)(2,1)S(1)} %get-tuple-element.354) | copy-start | bytes 393220
  289.6 8.1 %copy-start.19 = (bf16[512,1,128]{2,0,1:T(8,128)(2,1)}, bf16[512,1,128]{2,0,1:T(8,128)(2,1)S(1)}, u32[]{:S(2)}) copy-start(bf16[512,1,128]{2,0,1:T(8,128)(2,1)S(1)} %get-tuple-element.353) | copy-start | bytes 393220
  (35 other events, 68.2 us)
Sparse Core Ops, SparseCore 0:
  223.5 65.0 reduce-scatter.2
  313.7 70.6 reduce-scatter.4
